TPU v7x, 256 devices: a whole 4x4x8 slice. The times are simulated.
256 devices in a mesh: dp: 2 (over y_hi), context: 16 (over y_lo, z), tensor: 8 (over x, core).
Axes of the slice: x: 4, y: 4 (y_hi: 2, y_lo: 2; y = y_hi * 2 + y_lo), z: 8, core: 2. Of those that a mesh axis runs over, the one named last changes fastest.
Arguments:
- queries: bfloat16 [8192, 8192], P(('dp', 'context'), 'tensor'), parts along dimension 0, may hold values from -6 to 6
- keys: bfloat16 [8192, 1024], P(('dp', 'context'), 'tensor'), parts along dimension 0, may hold values from -12 to 12
- values: bfloat16 [8192, 1024], P(('dp', 'context'), 'tensor'), parts along dimension 0, may hold values from -6 to 6
- span_order: int32 [64], P('dp'), parts along dimension 0, may hold values from 0 to 31, each once
- out_weight: bfloat16 [8192, 4096], P('tensor'), may hold values from -0.25 to 0.25
Outputs:
- projected: bfloat16 [8192, 4096], P(('dp', 'context', 'tensor')), parts along dimension 0
There are 2 independent parts, one for each index of `dp`. A program takes and returns all parts, laid end to end along the dimension named above; an argument that names none is the same for every part. Nothing has to cross between parts.
All inputs are finite; a program needn't handle non-finite values.
Results may differ from a plain program's by a relative error of at most 0.02.
Values may be sent and summed in bfloat16 or wider, within the bound.
A program may use at most 64 MiB of HBM per device.

v0:
```python
import math

import jax
import jax.numpy as jnp
from jax import lax
from jax.experimental import pallas as pl
from jax.experimental.pallas import tpu as pltpu
from jax.sharding import PartitionSpec as P

HEAD_DIM = 128
SPAN = 128
RING = 8
COLUMNS = 2
CHIPS = 4
ROUNDS = 10
TILE = 512
TILES = 8
HALF = TILES // 2
LOWEST = -1e30
MESH = pl.DeviceIdType.MESH

UP = [(0, 1, 0), (0, 1, 1), (0, 2, 0), (0, 2, 1), (0, 3, 0), (0, 3, 1),
      (1, 3, 0), (0, 4, 0), (1, 4, 0), (1, 3, 1)]
DOWN = [(0, -1, 1), (0, -1, 0), (0, -2, 1), (0, -2, 0), (0, -3, 1), (0, -3, 0),
        (0, -4, 1), (1, -3, 1), (1, -3, 0), (1, -4, 1)]
ACROSS = [(1, 0, 0), (1, 0, 1), (1, 1, 0), (1, -1, 1), (1, 2, 0), (1, -2, 1),
          (1, -2, 0), (1, 2, 1), (1, 1, 1), (1, -1, 0)]


def plan():
    slot_of = {(0, 0, 0): 0, (0, 0, 1): 1}
    contents = [(0, 0, 0), (0, 0, 1)]
    up_slot = {r: 2 + 3 * r for r in range(ROUNDS)}
    down_slot = {r: 3 + 3 * r for r in range(ROUNDS)}
    across_slot = {r: 4 + 3 * r for r in range(ROUNDS)}
    slots = {}
    for r in range(ROUNDS):
        for table, names in ((up_slot, UP), (down_slot, DOWN), (across_slot, ACROSS)):
            slots[table[r]] = names[r]
    for slot in range(2, 2 + 3 * ROUNDS):
        column, offset, half = slots[slot]
        key = (column, offset % RING, half)
        slot_of[key] = slot
        contents.append(key)
    assert len(slot_of) == 2 + 3 * ROUNDS
    copies = []
    for r in range(ROUNDS):
        (uc, uo, uh), (dc, do, dh), (ac, ao, ah) = UP[r], DOWN[r], ACROSS[r]
        copies.append((
            ("minus", slot_of[(uc, (uo - 1) % RING, uh)], up_slot[r]),
            ("plus", slot_of[(dc, (do + 1) % RING, dh)], down_slot[r]),
            ("other", slot_of[(0, ao % RING, ah)], across_slot[r]),
        ))
    return contents, copies


CONTENTS, COPIES = plan()
SPANS = len(CONTENTS)
ORDER = tuple(part * HALF + tile for tile in range(HALF) for part in range(2))


def kernel(order_hbm, q_hbm, k_hbm, v_hbm, w_hbm, out,
           q_in, kv, w, qt, acc, top, att, own, sib_out, sib_in,
           far_out, far_in, near_out, near_in, result, order, span_of,
           load_sem, own_send, own_recv, kv_send, kv_recv, sib_send, sib_recv,
           far_send, far_recv, near_send, near_recv, out_sem):
    heads = q_in.shape[1] // HEAD_DIM
    rows = q_in.shape[0]
    context = lax.axis_index("context")
    tensor = lax.axis_index("tensor")
    y, z = context // RING, lax.rem(context, RING)
    x, core = tensor // 2, lax.rem(tensor, 2)
    targets = {
        "minus": {"context": y * RING + lax.rem(z + RING - 1, RING)},
        "plus": {"context": y * RING + lax.rem(z + 1, RING)},
        "other": {"context": (1 - y) * RING + z},
    }
    sibling = {"tensor": x * 2 + 1 - core}
    chip_next, chip_back = lax.rem(x + 1, CHIPS), lax.rem(x + CHIPS - 1, CHIPS)
    chip_far = lax.rem(x + 2, CHIPS)
    to_next, to_back = {"tensor": chip_next * 2 + core}, {"tensor": chip_back * 2 + core}

    barrier = pltpu.get_barrier_semaphore()
    for target in (*targets.values(), sibling, to_next, to_back):
        pl.semaphore_signal(barrier, inc=1, device_id=target, device_id_type=MESH)

    loads = []
    for half in range(2):
        for part, source in enumerate((k_hbm, v_hbm)):
            loads.append(pltpu.make_async_copy(
                source.at[pl.ds(half * SPAN, SPAN)], kv.at[half, part],
                load_sem.at[2 * half + part]))
    chips = (chip_far, chip_next, chip_back, x)
    for group, chip in enumerate(chips):
        for part, owner in enumerate((core, 1 - core)):
            number = 2 * group + part
            first = pl.multiple_of(chip * 64 + owner * 32, 32)
            loads.append(pltpu.make_async_copy(
                q_hbm.at[pl.ds(first, 32)], q_in.at[pl.ds(32 * number, 32)],
                load_sem.at[4 + number]))
    loads.append(pltpu.make_async_copy(order_hbm, order, load_sem.at[13]))
    loads.append(pltpu.make_async_copy(w_hbm, w, load_sem.at[12]))
    for load in loads[:-1]:
        load.start()

    def own_copies(r):
        for name, src, dst in COPIES[r]:
            for part, source in enumerate((k_hbm, v_hbm)):
                yield pltpu.make_async_remote_copy(
                    src_ref=source.at[pl.ds(src * SPAN, SPAN)], dst_ref=kv.at[dst, part],
                    send_sem=own_send.at[dst - 2, part], recv_sem=own_recv.at[dst - 2, part],
                    device_id=targets[name], device_id_type=MESH)

    def copy_of(name, src, dst):
        return pltpu.make_async_remote_copy(
            src_ref=kv.at[src], dst_ref=kv.at[dst],
            send_sem=kv_send.at[dst - 8], recv_sem=kv_recv.at[dst - 8],
            device_id=targets[name], device_id_type=MESH)

    pl.semaphore_wait(barrier, 6)
    for copy in own_copies(0):
        copy.start()
    loads[-1].start()

    loads[12].wait()
    for slot, (column, offset, half) in enumerate(CONTENTS):
        where = (y if column == 0 else 1 - y) * RING + lax.rem(z + offset, RING)
        span_of[slot] = order[2 * where + half]

    scale = math.log2(math.e) / math.sqrt(HEAD_DIM)
    for load in loads[4:12]:
        load.wait()
    for head in range(heads):
        scaled = q_in[:, head * HEAD_DIM:(head + 1) * HEAD_DIM].astype(jnp.float32).T * scale
        high = scaled.astype(jnp.bfloat16)
        low = (scaled - high.astype(jnp.float32)).astype(jnp.bfloat16)
        qt[head, :HEAD_DIM] = high
        qt[head, HEAD_DIM:] = low

    for first, second in zip(own_copies(0), own_copies(1)):
        first.wait_send()
        second.start()
    for load in loads[:4]:
        load.wait()

    lane = lax.broadcasted_iota(jnp.int32, (1, rows), 1)
    group_of = lane // 64
    chip_of = jnp.where(group_of == 0, chip_far, jnp.where(
        group_of == 1, chip_next, jnp.where(group_of == 2, chip_back, x)))
    owner_of = jnp.where(lax.rem(lane // 32, 2) == 0, core, 1 - core)
    row_of = chip_of * 64 + owner_of * 32 + lax.rem(lane, 32)
    q_span = jnp.where(row_of < SPAN, span_of[0], span_of[1])
    q_pos = q_span * SPAN + lax.rem(row_of, SPAN)

    def operands(first, count):
        spans = kv[pl.ds(first, count)]
        keys = spans[:, 0].reshape(count * SPAN, HEAD_DIM)
        keys = jnp.concatenate([keys, keys], axis=1)
        values = spans[:, 1].reshape(count * SPAN, HEAD_DIM).T
        ones = jnp.ones((16, count * SPAN), jnp.bfloat16)
        return keys, jnp.concatenate([values, ones], axis=0)

    def scores_of(keys, head):
        return jnp.dot(keys, qt[head], preferred_element_type=jnp.float32)

    def receive(r):
        following = COPIES[r + 2] if r + 2 < ROUNDS else ()
        here = 2 + 3 * r
        for copy in following:
            if copy[1] < here:
                copy_of(*copy).start()
        first = list(own_copies(r)) if r < 2 else ()
        for number, copy in enumerate(COPIES[r]):
            if r < 2:
                first[2 * number].wait_recv()
                first[2 * number + 1].wait_recv()
            else:
                copy_of(*copy).wait_recv()
            for later in following:
                if later[1] == copy[2]:
                    copy_of(*later).start()

    keys, values = operands(0, 2)
    k_row = lax.broadcasted_iota(jnp.int32, (2 * SPAN, 1), 0)
    k_pos = jnp.where(k_row < SPAN, span_of[0], span_of[1]) * SPAN + lax.rem(k_row, SPAN)
    hide = jnp.where(k_pos <= q_pos, 0.0, LOWEST)
    following = scores_of(keys, 0)
    for head in range(heads):
        scores = following + hide
        if head + 1 < heads:
            following = scores_of(keys, head + 1)
        new_top = jnp.max(scores, axis=0, keepdims=True)
        weights = jnp.exp2(scores - new_top).astype(jnp.bfloat16)
        top[head] = new_top
        acc[head] = jnp.dot(values, weights, preferred_element_type=jnp.float32)

    @pl.loop(0, ROUNDS)
    def _(step):
        for r in range(ROUNDS):
            @pl.when(step == r)
            def _():
                receive(r)

        first = 2 + 3 * step
        keys, values = operands(first, 3)
        hide = [jnp.where(span_of[first + number] < q_span, 0.0, LOWEST) for number in range(3)]
        following = scores_of(keys, 0)
        for head in range(heads):
            scores = [following[number * SPAN:(number + 1) * SPAN] for number in range(3)]
            if head + 1 < heads:
                following = scores_of(keys, head + 1)
            old_top = top[head]
            new_top = old_top
            for part, hidden in zip(scores, hide):
                new_top = jnp.maximum(new_top, jnp.max(part, axis=0, keepdims=True) + hidden)
            factor = jnp.exp2(old_top - new_top)
            weights = jnp.concatenate([
                jnp.exp2(part - (new_top - hidden)).astype(jnp.bfloat16)
                for part, hidden in zip(scores, hide)], axis=0)
            top[head] = new_top
            acc[head] = acc[head] * factor + jnp.dot(
                values, weights, preferred_element_type=jnp.float32)

    for head in range(heads):
        mixed = acc[head, :HEAD_DIM] * (1.0 / acc[head, HEAD_DIM:HEAD_DIM + 1])
        att[:, head * HEAD_DIM:(head + 1) * HEAD_DIM] = mixed.astype(jnp.bfloat16).T
    loads[13].wait()

    def sib_copy(tile, part):
        at = 0 if part == 0 else pl.ds(1, 3)
        return pltpu.make_async_remote_copy(
            src_ref=sib_out.at[tile, at], dst_ref=sib_in.at[tile, at],
            send_sem=sib_send.at[tile, part], recv_sem=sib_recv.at[tile, part],
            device_id=sibling, device_id_type=MESH)

    def project(tile):
        part = jnp.dot(att[...], w[:, tile * TILE:(tile + 1) * TILE],
                       preferred_element_type=jnp.float32).astype(jnp.bfloat16)
        part = part.reshape(4, 2, 32, TILE)
        sib_out[tile] = part[:, 1]
        sib_copy(tile, 0).start()
        sib_copy(tile, 1).start()
        own[tile] = part[:, 0]

    def both(tile, group):
        return own[tile, group].astype(jnp.float32) + sib_in[tile, group].astype(jnp.float32)

    def far_copy(tile):
        return pltpu.make_async_remote_copy(
            src_ref=far_out.at[tile], dst_ref=far_in.at[tile],
            send_sem=far_send.at[tile], recv_sem=far_recv.at[tile],
            device_id=to_next if tile < HALF else to_back, device_id_type=MESH)

    def near_copy(side, tile):
        return pltpu.make_async_remote_copy(
            src_ref=near_out.at[side, tile], dst_ref=near_in.at[side, tile],
            send_sem=near_send.at[side, tile], recv_sem=near_recv.at[side, tile],
            device_id=to_next if side == 0 else to_back, device_id_type=MESH)

    def out_copy(tile):
        at = pl.ds(tile * TILE, TILE)
        return pltpu.make_async_copy(result.at[:, at], out.at[:, at], out_sem.at[tile])

    def send_far(tile):
        sib_copy(tile, 0).wait_recv()
        far_out[tile] = both(tile, 0).astype(jnp.bfloat16)
        far_copy(tile).start()

    def send_near(side, tile):
        second = (tile < HALF) == (side == 0)
        if not second:
            sib_copy(tile, 1).wait_recv()
        total = both(tile, 1 + side)
        if second:
            far_copy(tile).wait_recv()
            total = total + far_in[tile].astype(jnp.float32)
        near_out[side, tile] = total.astype(jnp.bfloat16)
        near_copy(side, tile).start()

    project(ORDER[0])
    for earlier, tile in zip(ORDER, ORDER[1:]):
        project(tile)
        send_far(earlier)
    send_far(ORDER[-1])
    for tile in ORDER:
        send_near(0 if tile >= HALF else 1, tile)
    for tile in ORDER:
        send_near(0 if tile < HALF else 1, tile)
    for tile in ORDER:
        near_copy(0, tile).wait_recv()
        near_copy(1, tile).wait_recv()
        total = both(tile, 3) + (near_in[0, tile].astype(jnp.float32)
                                 + near_in[1, tile].astype(jnp.float32))
        result[:, tile * TILE:(tile + 1) * TILE] = total.astype(out.dtype)
        out_copy(tile).start()

    for copy in own_copies(1):
        copy.wait_send()
    for copies in COPIES[2:]:
        for copy in copies:
            copy_of(*copy).wait_send()
    for tile in range(TILES):
        for part in range(2):
            sib_copy(tile, part).wait_send()
            near_copy(part, tile).wait_send()
        far_copy(tile).wait_send()
        out_copy(tile).wait()


def on_device(queries, keys, values, span_order, out_weight):
    rows, width = queries.shape
    heads = width // HEAD_DIM
    d_out = out_weight.shape[1]
    bf16, f32 = jnp.bfloat16, jnp.float32
    sem = pltpu.SemaphoreType.DMA
    span_order, queries, keys, values, out_weight = (
        pltpu.with_memory_space_constraint(array, pltpu.HBM)
        for array in (span_order, queries, keys, values, out_weight))
    return pl.pallas_call(
        kernel,
        out_shape=jax.ShapeDtypeStruct((rows // 8, d_out), bf16),
        in_specs=[pl.BlockSpec(memory_space=pltpu.HBM)] * 5,
        out_specs=pl.BlockSpec(memory_space=pl.ANY),
        scratch_shapes=[
            pltpu.VMEM((rows, width), bf16),
            pltpu.VMEM((SPANS, 2, SPAN, HEAD_DIM), bf16),
            pltpu.VMEM((width, d_out), bf16),
            pltpu.VMEM((heads, 2 * HEAD_DIM, rows), bf16),
            pltpu.VMEM((heads, HEAD_DIM + 16, rows), f32),
            pltpu.VMEM((heads, 1, rows), f32),
            pltpu.VMEM((rows, width), bf16),
            pltpu.VMEM((TILES, 4, 32, TILE), bf16),
            pltpu.VMEM((TILES, 4, 32, TILE), bf16),
            pltpu.VMEM((TILES, 4, 32, TILE), bf16),
            pltpu.VMEM((TILES, 32, TILE), bf16),
            pltpu.VMEM((TILES, 32, TILE), bf16),
            pltpu.VMEM((2, TILES, 32, TILE), bf16),
            pltpu.VMEM((2, TILES, 32, TILE), bf16),
            pltpu.VMEM((rows // 8, d_out), bf16),
            pltpu.SMEM((SPANS,), jnp.int32),
            pltpu.SMEM((SPANS,), jnp.int32),
            sem((14,)), sem((6, 2)), sem((6, 2)), sem((SPANS - 8,)), sem((SPANS - 8,)),
            sem((TILES, 2)), sem((TILES, 2)), sem((TILES,)), sem((TILES,)),
            sem((2, TILES)), sem((2, TILES)), sem((TILES,)),
        ],
        compiler_params=pltpu.CompilerParams(
            collective_id=0, has_side_effects=True, vmem_limit_bytes=32 * 1024 * 1024),
        cost_estimate=pl.CostEstimate(
            flops=3 * 2 * rows * width * 4096, bytes_accessed=10 * 2**20,
            transcendentals=heads * rows * 4096),
    )(span_order, queries, keys, values, out_weight)


def solution(mesh):
    return jax.shard_map(
        on_device,
        mesh=mesh,
        in_specs=(
            P(("dp", "context"), "tensor"),
            P(("dp", "context"), "tensor"),
            P(("dp", "context"), "tensor"),
            P("dp"),
            P("tensor", None),
        ),
        out_specs=P(("dp", "context", "tensor"), None),
        check_vma=False,
    )
```

profile of v0, /device:TPU:1, one launch (start us, length us, event | category | flops | bytes accessed | tf_op | source)
XLA Modules:
  0.0 48.8 jit_solution(1638925679752330989)
XLA Ops:
  0.0 48.1 %shard_map.55 = bf16[32,4096]{1,0:T(8,128)(2,1)S(1)} custom-call(s32[32]{0:T(128)} %order_hbm.1, bf16[256,1024]{1,0:T(8,128)(2,1)} %q_hbm.1, bf16[256,128]{1,0:T(8,128)(2,1)} %k_hbm.1, bf16[256,128]{1,0:T(8,128)(2,1)} %v_hbm.1, bf16[1024,4096]{1,0:T(8,128)(2,1)} %w_hbm.1), custom_call_target="tpu_custom_call" | custom-call | flops 6442450944 | bytes 10485760 | tf_op jit(solution)/shard_map/pallas_call | solution.py:319
  48.1 0.7 %copy.7 = bf16[32,4096]{1,0:T(8,128)(2,1)} copy(bf16[32,4096]{1,0:T(8,128)(2,1)S(1)} %shard_map.55) | data formatting | bytes 524288
where the time goes:
time: 48.9 us; the launch traced here: 48.8 us
  Pallas kernels  48.1 us (98%)
  local copies, waits for them, and re-layouts  0.71 us (1%)
    pallas_call x1, Pallas kernels, on_device(): pl.pallas_call(kernel, out_shape=jax.ShapeDtypeStruct((rows // 8, d_out),...  48.1 us

commit v1 on v0

--- a/solution.py
+++ b/solution.py
@@ -277,13 +277,15 @@
         near_out[side, tile] = total.astype(jnp.bfloat16)
         near_copy(side, tile).start()
 
+    def send_first(tile):
+        send_far(tile)
+        send_near(0 if tile >= HALF else 1, tile)
+
     project(ORDER[0])
     for earlier, tile in zip(ORDER, ORDER[1:]):
         project(tile)
-        send_far(earlier)
-    send_far(ORDER[-1])
-    for tile in ORDER:
-        send_near(0 if tile >= HALF else 1, tile)
+        send_first(earlier)
+    send_first(ORDER[-1])
     for tile in ORDER:
         send_near(0 if tile < HALF else 1, tile)
     for tile in ORDER:

time: 48.9 us -> 47.4 us (0.969)
  Pallas kernels: 48.1 us -> 46.6 us
    pallas_call x1, Pallas kernels: 48.1 us -> 46.6 us  [on_device(): pl.pallas_call(kernel, out_shape=jax.ShapeDtypeStruct((rows // 8, d_out),...]
where the time goes in v1:
time: 47.4 us; the launch traced here: 47.3 us
  Pallas kernels  46.6 us (98%)
  local copies, waits for them, and re-layouts  0.71 us (1%)
    pallas_call x1, Pallas kernels, on_device(): pl.pallas_call(kernel, out_shape=jax.ShapeDtypeStruct((rows // 8, d_out),...  46.6 us

profile of v1, /device:TPU:1, one launch (start us, length us, event | category | flops | bytes accessed | tf_op | source)
XLA Modules:
  0.0 47.3 jit_solution(16212718692857024635)
XLA Ops:
  0.0 46.6 %shard_map.55 = bf16[32,4096]{1,0:T(8,128)(2,1)S(1)} custom-call(s32[32]{0:T(128)} %order_hbm.1, bf16[256,1024]{1,0:T(8,128)(2,1)} %q_hbm.1, bf16[256,128]{1,0:T(8,128)(2,1)} %k_hbm.1, bf16[256,128]{1,0:T(8,128)(2,1)} %v_hbm.1, bf16[1024,4096]{1,0:T(8,128)(2,1)} %w_hbm.1), custom_call_target="tpu_custom_call" | custom-call | flops 6442450944 | bytes 10485760 | tf_op jit(solution)/shard_map/pallas_call | solution.py:321
  46.6 0.7 %copy.7 = bf16[32,4096]{1,0:T(8,128)(2,1)} copy(bf16[32,4096]{1,0:T(8,128)(2,1)S(1)} %shard_map.55) | data formatting | bytes 524288

commit v2 on v1

--- a/solution.py
+++ b/solution.py
@@ -127,15 +127,10 @@
         where = (y if column == 0 else 1 - y) * RING + lax.rem(z + offset, RING)
         span_of[slot] = order[2 * where + half]
 
-    scale = math.log2(math.e) / math.sqrt(HEAD_DIM)
     for load in loads[4:12]:
         load.wait()
     for head in range(heads):
-        scaled = q_in[:, head * HEAD_DIM:(head + 1) * HEAD_DIM].astype(jnp.float32).T * scale
-        high = scaled.astype(jnp.bfloat16)
-        low = (scaled - high.astype(jnp.float32)).astype(jnp.bfloat16)
-        qt[head, :HEAD_DIM] = high
-        qt[head, HEAD_DIM:] = low
+        qt[head] = q_in[:, head * HEAD_DIM:(head + 1) * HEAD_DIM].T
 
     for first, second in zip(own_copies(0), own_copies(1)):
         first.wait_send()
@@ -155,10 +150,11 @@
     def operands(first, count):
         spans = kv[pl.ds(first, count)]
         keys = spans[:, 0].reshape(count * SPAN, HEAD_DIM)
-        keys = jnp.concatenate([keys, keys], axis=1)
         values = spans[:, 1].reshape(count * SPAN, HEAD_DIM).T
         ones = jnp.ones((16, count * SPAN), jnp.bfloat16)
         return keys, jnp.concatenate([values, ones], axis=0)
+
+    scale = math.log2(math.e) / math.sqrt(HEAD_DIM)
 
     def scores_of(keys, head):
         return jnp.dot(keys, qt[head], preferred_element_type=jnp.float32)
@@ -186,7 +182,7 @@
     hide = jnp.where(k_pos <= q_pos, 0.0, LOWEST)
     following = scores_of(keys, 0)
     for head in range(heads):
-        scores = following + hide
+        scores = following * scale + hide
         if head + 1 < heads:
             following = scores_of(keys, head + 1)
         new_top = jnp.max(scores, axis=0, keepdims=True)
@@ -212,10 +208,10 @@
             old_top = top[head]
             new_top = old_top
             for part, hidden in zip(scores, hide):
-                new_top = jnp.maximum(new_top, jnp.max(part, axis=0, keepdims=True) + hidden)
+                new_top = jnp.maximum(new_top, jnp.max(part, axis=0, keepdims=True) * scale + hidden)
             factor = jnp.exp2(old_top - new_top)
             weights = jnp.concatenate([
-                jnp.exp2(part - (new_top - hidden)).astype(jnp.bfloat16)
+                jnp.exp2(part * scale - (new_top - hidden)).astype(jnp.bfloat16)
                 for part, hidden in zip(scores, hide)], axis=0)
             top[head] = new_top
             acc[head] = acc[head] * factor + jnp.dot(
@@ -327,7 +323,7 @@
             pltpu.VMEM((rows, width), bf16),
             pltpu.VMEM((SPANS, 2, SPAN, HEAD_DIM), bf16),
             pltpu.VMEM((width, d_out), bf16),
-            pltpu.VMEM((heads, 2 * HEAD_DIM, rows), bf16),
+            pltpu.VMEM((heads, HEAD_DIM, rows), bf16),
             pltpu.VMEM((heads, HEAD_DIM + 16, rows), f32),
             pltpu.VMEM((heads, 1, rows), f32),
             pltpu.VMEM((rows, width), bf16),

time: 47.4 us -> 46.3 us (0.977)
  Pallas kernels: 46.6 us -> 45.4 us
    pallas_call x1, Pallas kernels: 46.6 us -> 45.4 us  [on_device(): pl.pallas_call(kernel, out_shape=jax.ShapeDtypeStruct((rows // 8, d_out),...]
where the time goes in v2:
time: 46.3 us; the launch traced here: 46.1 us
  Pallas kernels  45.4 us (98%)
  local copies, waits for them, and re-layouts  0.71 us (2%)
    pallas_call x1, Pallas kernels, on_device(): pl.pallas_call(kernel, out_shape=jax.ShapeDtypeStruct((rows // 8, d_out),...  45.4 us

profile of v2, /device:TPU:1, one launch (start us, length us, event | category | flops | bytes accessed | tf_op | source)
XLA Modules:
  0.0 46.1 jit_solution(1422036035489796521)
XLA Ops:
  0.0 45.4 %shard_map.55 = bf16[32,4096]{1,0:T(8,128)(2,1)S(1)} custom-call(s32[32]{0:T(128)} %order_hbm.1, bf16[256,1024]{1,0:T(8,128)(2,1)} %q_hbm.1, bf16[256,128]{1,0:T(8,128)(2,1)} %k_hbm.1, bf16[256,128]{1,0:T(8,128)(2,1)} %v_hbm.1, bf16[1024,4096]{1,0:T(8,128)(2,1)} %w_hbm.1), custom_call_target="tpu_custom_call" | custom-call | flops 6442450944 | bytes 10485760 | tf_op jit(solution)/shard_map/pallas_call | solution.py:317
  45.4 0.7 %copy.7 = bf16[32,4096]{1,0:T(8,128)(2,1)} copy(bf16[32,4096]{1,0:T(8,128)(2,1)S(1)} %shard_map.55) | data formatting | bytes 524288

commit v3 on v2

--- a/solution.py
+++ b/solution.py
@@ -186,7 +186,7 @@
         if head + 1 < heads:
             following = scores_of(keys, head + 1)
         new_top = jnp.max(scores, axis=0, keepdims=True)
-        weights = jnp.exp2(scores - new_top).astype(jnp.bfloat16)
+        weights = jnp.exp2((scores - new_top).astype(jnp.bfloat16))
         top[head] = new_top
         acc[head] = jnp.dot(values, weights, preferred_element_type=jnp.float32)
 
@@ -211,7 +211,7 @@
                 new_top = jnp.maximum(new_top, jnp.max(part, axis=0, keepdims=True) * scale + hidden)
             factor = jnp.exp2(old_top - new_top)
             weights = jnp.concatenate([
-                jnp.exp2(part * scale - (new_top - hidden)).astype(jnp.bfloat16)
+                jnp.exp2((part * scale - (new_top - hidden)).astype(jnp.bfloat16))
                 for part, hidden in zip(scores, hide)], axis=0)
             top[head] = new_top
             acc[head] = acc[head] * factor + jnp.dot(

time: 46.3 us -> 46.3 us (level)
  no operation moved by 1% of the time
where the time goes in v3:
time: 46.3 us; the launch traced here: 46.2 us
  Pallas kernels  45.4 us (98%)
  local copies, waits for them, and re-layouts  0.71 us (2%)
    pallas_call x1, Pallas kernels, on_device(): pl.pallas_call(kernel, out_shape=jax.ShapeDtypeStruct((rows // 8, d_out),...  45.4 us

profile of v3, /device:TPU:1, one launch (start us, length us, event | category | flops | bytes accessed | tf_op | source)
XLA Modules:
  0.0 46.2 jit_solution(2331492583123408141)
XLA Ops:
  0.0 45.4 %shard_map.55 = bf16[32,4096]{1,0:T(8,128)(2,1)S(1)} custom-call(s32[32]{0:T(128)} %order_hbm.1, bf16[256,1024]{1,0:T(8,128)(2,1)} %q_hbm.1, bf16[256,128]{1,0:T(8,128)(2,1)} %k_hbm.1, bf16[256,128]{1,0:T(8,128)(2,1)} %v_hbm.1, bf16[1024,4096]{1,0:T(8,128)(2,1)} %w_hbm.1), custom_call_target="tpu_custom_call" | custom-call | flops 6442450944 | bytes 10485760 | tf_op jit(solution)/shard_map/pallas_call | solution.py:317
  45.5 0.7 %copy.7 = bf16[32,4096]{1,0:T(8,128)(2,1)} copy(bf16[32,4096]{1,0:T(8,128)(2,1)S(1)} %shard_map.55) | data formatting | bytes 524288

commit v4 on v2

--- a/solution.py
+++ b/solution.py
@@ -15,7 +15,6 @@
 ROUNDS = 10
 TILE = 512
 TILES = 8
-HALF = TILES // 2
 LOWEST = -1e30
 MESH = pl.DeviceIdType.MESH
 
@@ -56,7 +55,7 @@
 
 CONTENTS, COPIES = plan()
 SPANS = len(CONTENTS)
-ORDER = tuple(part * HALF + tile for tile in range(HALF) for part in range(2))
+GROUPS = ((0, 1), (4, 1), (1, 1), (5, 1), (2, 2), (6, 2))
 
 
 def kernel(order_hbm, q_hbm, k_hbm, v_hbm, w_hbm, out,
@@ -222,86 +221,93 @@
         att[:, head * HEAD_DIM:(head + 1) * HEAD_DIM] = mixed.astype(jnp.bfloat16).T
     loads[13].wait()
 
-    def sib_copy(tile, part):
-        at = 0 if part == 0 else pl.ds(1, 3)
+    def sib_copy(group):
+        at = pl.ds(*GROUPS[group])
         return pltpu.make_async_remote_copy(
-            src_ref=sib_out.at[tile, at], dst_ref=sib_in.at[tile, at],
-            send_sem=sib_send.at[tile, part], recv_sem=sib_recv.at[tile, part],
+            src_ref=sib_out.at[at], dst_ref=sib_in.at[at],
+            send_sem=sib_send.at[group], recv_sem=sib_recv.at[group],
             device_id=sibling, device_id_type=MESH)
 
-    def project(tile):
-        part = jnp.dot(att[...], w[:, tile * TILE:(tile + 1) * TILE],
-                       preferred_element_type=jnp.float32).astype(jnp.bfloat16)
-        part = part.reshape(4, 2, 32, TILE)
-        sib_out[tile] = part[:, 1]
-        sib_copy(tile, 0).start()
-        sib_copy(tile, 1).start()
-        own[tile] = part[:, 0]
-
-    def both(tile, group):
-        return own[tile, group].astype(jnp.float32) + sib_in[tile, group].astype(jnp.float32)
-
-    def far_copy(tile):
+    def tiles_of(group):
+        first, count = GROUPS[group]
+        return range(first, first + count)
+
+    def project(group):
+        for tile in tiles_of(group):
+            part = jnp.dot(att[...], w[:, tile * TILE:(tile + 1) * TILE],
+                           preferred_element_type=jnp.float32).astype(jnp.bfloat16)
+            part = part.reshape(4, 2, 32, TILE)
+            sib_out[tile] = part[:, 1]
+            own[tile] = part[:, 0]
+        sib_copy(group).start()
+
+    def both(tile, owner):
+        return own[tile, owner].astype(jnp.float32) + sib_in[tile, owner].astype(jnp.float32)
+
+    def far_copy(group):
+        at = pl.ds(*GROUPS[group])
         return pltpu.make_async_remote_copy(
-            src_ref=far_out.at[tile], dst_ref=far_in.at[tile],
-            send_sem=far_send.at[tile], recv_sem=far_recv.at[tile],
-            device_id=to_next if tile < HALF else to_back, device_id_type=MESH)
-
-    def near_copy(side, tile):
+            src_ref=far_out.at[at], dst_ref=far_in.at[at],
+            send_sem=far_send.at[group], recv_sem=far_recv.at[group],
+            device_id=to_next if group % 2 == 0 else to_back, device_id_type=MESH)
+
+    def near_copy(side, group):
+        at = pl.ds(*GROUPS[group])
         return pltpu.make_async_remote_copy(
-            src_ref=near_out.at[side, tile], dst_ref=near_in.at[side, tile],
-            send_sem=near_send.at[side, tile], recv_sem=near_recv.at[side, tile],
+            src_ref=near_out.at[side, at], dst_ref=near_in.at[side, at],
+            send_sem=near_send.at[side, group], recv_sem=near_recv.at[side, group],
             device_id=to_next if side == 0 else to_back, device_id_type=MESH)
 
     def out_copy(tile):
         at = pl.ds(tile * TILE, TILE)
         return pltpu.make_async_copy(result.at[:, at], out.at[:, at], out_sem.at[tile])
 
-    def send_far(tile):
-        sib_copy(tile, 0).wait_recv()
-        far_out[tile] = both(tile, 0).astype(jnp.bfloat16)
-        far_copy(tile).start()
-
-    def send_near(side, tile):
-        second = (tile < HALF) == (side == 0)
-        if not second:
-            sib_copy(tile, 1).wait_recv()
-        total = both(tile, 1 + side)
-        if second:
-            far_copy(tile).wait_recv()
-            total = total + far_in[tile].astype(jnp.float32)
-        near_out[side, tile] = total.astype(jnp.bfloat16)
-        near_copy(side, tile).start()
-
-    def send_first(tile):
-        send_far(tile)
-        send_near(0 if tile >= HALF else 1, tile)
-
-    project(ORDER[0])
-    for earlier, tile in zip(ORDER, ORDER[1:]):
-        project(tile)
-        send_first(earlier)
-    send_first(ORDER[-1])
-    for tile in ORDER:
-        send_near(0 if tile < HALF else 1, tile)
-    for tile in ORDER:
-        near_copy(0, tile).wait_recv()
-        near_copy(1, tile).wait_recv()
-        total = both(tile, 3) + (near_in[0, tile].astype(jnp.float32)
-                                 + near_in[1, tile].astype(jnp.float32))
-        result[:, tile * TILE:(tile + 1) * TILE] = total.astype(out.dtype)
-        out_copy(tile).start()
+    def send_first(group):
+        sib_copy(group).wait_recv()
+        side = 1 - group % 2
+        for tile in tiles_of(group):
+            far_out[tile] = both(tile, 0).astype(jnp.bfloat16)
+        far_copy(group).start()
+        for tile in tiles_of(group):
+            near_out[side, tile] = both(tile, 1 + side).astype(jnp.bfloat16)
+        near_copy(side, group).start()
+
+    def send_second(group):
+        side = group % 2
+        far_copy(group).wait_recv()
+        for tile in tiles_of(group):
+            total = both(tile, 1 + side) + far_in[tile].astype(jnp.float32)
+            near_out[side, tile] = total.astype(jnp.bfloat16)
+        near_copy(side, group).start()
+
+    count = len(GROUPS)
+    project(0)
+    for group in range(1, count):
+        project(group)
+        send_first(group - 1)
+    send_first(count - 1)
+    for group in range(count):
+        send_second(group)
+    for group in range(count):
+        near_copy(0, group).wait_recv()
+        near_copy(1, group).wait_recv()
+        for tile in tiles_of(group):
+            total = both(tile, 3) + (near_in[0, tile].astype(jnp.float32)
+                                     + near_in[1, tile].astype(jnp.float32))
+            result[:, tile * TILE:(tile + 1) * TILE] = total.astype(out.dtype)
+            out_copy(tile).start()
 
     for copy in own_copies(1):
         copy.wait_send()
     for copies in COPIES[2:]:
         for copy in copies:
             copy_of(*copy).wait_send()
+    for group in range(count):
+        sib_copy(group).wait_send()
+        far_copy(group).wait_send()
+        for side in range(2):
+            near_copy(side, group).wait_send()
     for tile in range(TILES):
-        for part in range(2):
-            sib_copy(tile, part).wait_send()
-            near_copy(part, tile).wait_send()
-        far_copy(tile).wait_send()
         out_copy(tile).wait()
 
 
@@ -311,6 +317,7 @@
     d_out = out_weight.shape[1]
     bf16, f32 = jnp.bfloat16, jnp.float32
     sem = pltpu.SemaphoreType.DMA
+    groups = len(GROUPS)
     span_order, queries, keys, values, out_weight = (
         pltpu.with_memory_space_constraint(array, pltpu.HBM)
         for array in (span_order, queries, keys, values, out_weight))
@@ -338,8 +345,8 @@
             pltpu.SMEM((SPANS,), jnp.int32),
             pltpu.SMEM((SPANS,), jnp.int32),
             sem((14,)), sem((6, 2)), sem((6, 2)), sem((SPANS - 8,)), sem((SPANS - 8,)),
-            sem((TILES, 2)), sem((TILES, 2)), sem((TILES,)), sem((TILES,)),
-            sem((2, TILES)), sem((2, TILES)), sem((TILES,)),
+            sem((groups,)), sem((groups,)), sem((groups,)), sem((groups,)),
+            sem((2, groups)), sem((2, groups)), sem((TILES,)),
         ],
         compiler_params=pltpu.CompilerParams(
             collective_id=0, has_side_effects=True, vmem_limit_bytes=32 * 1024 * 1024),

time: 46.3 us -> 47.1 us (1.017)
  Pallas kernels: 45.4 us -> 46.3 us
    pallas_call x1, Pallas kernels: 45.4 us -> 46.3 us  [on_device(): pl.pallas_call(kernel, out_shape=jax.ShapeDtypeStruct((rows // 8, d_out),...]
where the time goes in v4:
time: 47.1 us; the launch traced here: 47 us
  Pallas kernels  46.3 us (98%)
  local copies, waits for them, and re-layouts  0.71 us (2%)
    pallas_call x1, Pallas kernels, on_device(): pl.pallas_call(kernel, out_shape=jax.ShapeDtypeStruct((rows // 8, d_out),...  46.3 us

profile of v4, /device:TPU:1, one launch (start us, length us, event | category | flops | bytes accessed | tf_op | source)
XLA Modules:
  0.0 47.0 jit_solution(10227006794365729401)
XLA Ops:
  0.0 46.3 %shard_map.55 = bf16[32,4096]{1,0:T(8,128)(2,1)S(1)} custom-call(s32[32]{0:T(128)} %order_hbm.1, bf16[256,1024]{1,0:T(8,128)(2,1)} %q_hbm.1, bf16[256,128]{1,0:T(8,128)(2,1)} %k_hbm.1, bf16[256,128]{1,0:T(8,128)(2,1)} %v_hbm.1, bf16[1024,4096]{1,0:T(8,128)(2,1)} %w_hbm.1), custom_call_target="tpu_custom_call" | custom-call | flops 6442450944 | bytes 10485760 | tf_op jit(solution)/shard_map/pallas_call | solution.py:324
  46.3 0.7 %copy.7 = bf16[32,4096]{1,0:T(8,128)(2,1)} copy(bf16[32,4096]{1,0:T(8,128)(2,1)S(1)} %shard_map.55) | data formatting | bytes 524288

commit v5 on v2

--- a/solution.py
+++ b/solution.py
@@ -70,13 +70,14 @@
     tensor = lax.axis_index("tensor")
     y, z = context // RING, lax.rem(context, RING)
     x, core = tensor // 2, lax.rem(tensor, 2)
+    ahead = 1 - 2 * core
     targets = {
-        "minus": {"context": y * RING + lax.rem(z + RING - 1, RING)},
-        "plus": {"context": y * RING + lax.rem(z + 1, RING)},
+        "minus": {"context": y * RING + lax.rem(z + RING - ahead, RING)},
+        "plus": {"context": y * RING + lax.rem(z + RING + ahead, RING)},
         "other": {"context": (1 - y) * RING + z},
     }
     sibling = {"tensor": x * 2 + 1 - core}
-    chip_next, chip_back = lax.rem(x + 1, CHIPS), lax.rem(x + CHIPS - 1, CHIPS)
+    chip_next, chip_back = lax.rem(x + CHIPS + ahead, CHIPS), lax.rem(x + CHIPS - ahead, CHIPS)
     chip_far = lax.rem(x + 2, CHIPS)
     to_next, to_back = {"tensor": chip_next * 2 + core}, {"tensor": chip_back * 2 + core}
 
@@ -90,10 +91,11 @@
             loads.append(pltpu.make_async_copy(
                 source.at[pl.ds(half * SPAN, SPAN)], kv.at[half, part],
                 load_sem.at[2 * half + part]))
-    chips = (chip_far, chip_next, chip_back, x)
-    for group, chip in enumerate(chips):
+    chips = ((chip_far, chip_next, chip_back, x), (chip_far, chip_back, chip_next, x))
+    for group in range(4):
         for part, owner in enumerate((core, 1 - core)):
             number = 2 * group + part
+            chip = chips[part][group]
             first = pl.multiple_of(chip * 64 + owner * 32, 32)
             loads.append(pltpu.make_async_copy(
                 q_hbm.at[pl.ds(first, 32)], q_in.at[pl.ds(32 * number, 32)],
@@ -124,7 +126,7 @@
 
     loads[12].wait()
     for slot, (column, offset, half) in enumerate(CONTENTS):
-        where = (y if column == 0 else 1 - y) * RING + lax.rem(z + offset, RING)
+        where = (y if column == 0 else 1 - y) * RING + lax.rem(z + RING + ahead * offset, RING)
         span_of[slot] = order[2 * where + half]
 
     for load in loads[4:12]:
@@ -140,9 +142,10 @@
 
     lane = lax.broadcasted_iota(jnp.int32, (1, rows), 1)
     group_of = lane // 64
-    chip_of = jnp.where(group_of == 0, chip_far, jnp.where(
-        group_of == 1, chip_next, jnp.where(group_of == 2, chip_back, x)))
-    owner_of = jnp.where(lax.rem(lane // 32, 2) == 0, core, 1 - core)
+    mine = lax.rem(lane // 32, 2) == 0
+    chip_of = jnp.where(group_of == 0, chip_far, jnp.where(group_of == 3, x, jnp.where(
+        (group_of == 1) == mine, chip_next, chip_back)))
+    owner_of = jnp.where(mine, core, 1 - core)
     row_of = chip_of * 64 + owner_of * 32 + lax.rem(lane, 32)
     q_span = jnp.where(row_of < SPAN, span_of[0], span_of[1])
     q_pos = q_span * SPAN + lax.rem(row_of, SPAN)

time: 46.3 us -> 46.1 us (level)
  no operation moved by 1% of the time
where the time goes in v5:
time: 46.1 us; the launch traced here: 45.9 us
  Pallas kernels  45.2 us (98%)
  local copies, waits for them, and re-layouts  0.71 us (2%)
    pallas_call x1, Pallas kernels, on_device(): pl.pallas_call(kernel, out_shape=jax.ShapeDtypeStruct((rows // 8, d_out),...  45.2 us

profile of v5, /device:TPU:1, one launch (start us, length us, event | category | flops | bytes accessed | tf_op | source)
XLA Modules:
  0.0 45.9 jit_solution(8538256525153286062)
XLA Ops:
  0.0 45.2 %shard_map.55 = bf16[32,4096]{1,0:T(8,128)(2,1)S(1)} custom-call(s32[32]{0:T(128)} %order_hbm.1, bf16[256,1024]{1,0:T(8,128)(2,1)} %q_hbm.1, bf16[256,128]{1,0:T(8,128)(2,1)} %k_hbm.1, bf16[256,128]{1,0:T(8,128)(2,1)} %v_hbm.1, bf16[1024,4096]{1,0:T(8,128)(2,1)} %w_hbm.1), custom_call_target="tpu_custom_call" | custom-call | flops 6442450944 | bytes 10485760 | tf_op jit(solution)/shard_map/pallas_call | solution.py:320
  45.2 0.7 %copy.7 = bf16[32,4096]{1,0:T(8,128)(2,1)} copy(bf16[32,4096]{1,0:T(8,128)(2,1)S(1)} %shard_map.55) | data formatting | bytes 524288

commit v6 on v5

--- a/solution.py
+++ b/solution.py
@@ -193,13 +193,8 @@
         top[head] = new_top
         acc[head] = jnp.dot(values, weights, preferred_element_type=jnp.float32)
 
-    @pl.loop(0, ROUNDS)
-    def _(step):
-        for r in range(ROUNDS):
-            @pl.when(step == r)
-            def _():
-                receive(r)
-
+    for step in range(ROUNDS):
+        receive(step)
         first = 2 + 3 * step
         keys, values = operands(first, 3)
         hide = [jnp.where(span_of[first + number] < q_span, 0.0, LOWEST) for number in range(3)]

time: 46.1 us -> 46.5 us (level)
  no operation moved by 1% of the time
where the time goes in v6:
time: 46.5 us; the launch traced here: 46.4 us
  Pallas kernels  45.6 us (98%)
  local copies, waits for them, and re-layouts  0.71 us (2%)
    pallas_call x1, Pallas kernels, on_device(): pl.pallas_call(kernel, out_shape=jax.ShapeDtypeStruct((rows // 8, d_out),...  45.6 us

profile of v6, /device:TPU:1, one launch (start us, length us, event | category | flops | bytes accessed | tf_op | source)
XLA Modules:
  0.0 46.4 jit_solution(1454950514129279073)
XLA Ops:
  0.0 45.6 %shard_map.55 = bf16[32,4096]{1,0:T(8,128)(2,1)S(1)} custom-call(s32[32]{0:T(128)} %order_hbm.1, bf16[256,1024]{1,0:T(8,128)(2,1)} %q_hbm.1, bf16[256,128]{1,0:T(8,128)(2,1)} %k_hbm.1, bf16[256,128]{1,0:T(8,128)(2,1)} %v_hbm.1, bf16[1024,4096]{1,0:T(8,128)(2,1)} %w_hbm.1), custom_call_target="tpu_custom_call" | custom-call | flops 6442450944 | bytes 10485760 | tf_op jit(solution)/shard_map/pallas_call | solution.py:315
  45.6 0.7 %copy.7 = bf16[32,4096]{1,0:T(8,128)(2,1)} copy(bf16[32,4096]{1,0:T(8,128)(2,1)S(1)} %shard_map.55) | data formatting | bytes 524288

commit v7 on v5

--- a/solution.py
+++ b/solution.py
@@ -102,8 +102,6 @@
                 load_sem.at[4 + number]))
     loads.append(pltpu.make_async_copy(order_hbm, order, load_sem.at[13]))
     loads.append(pltpu.make_async_copy(w_hbm, w, load_sem.at[12]))
-    for load in loads[:-1]:
-        load.start()
 
     def own_copies(r):
         for name, src, dst in COPIES[r]:
@@ -122,7 +120,8 @@
     pl.semaphore_wait(barrier, 6)
     for copy in own_copies(0):
         copy.start()
-    loads[-1].start()
+    for load in loads:
+        load.start()
 
     loads[12].wait()
     for slot, (column, offset, half) in enumerate(CONTENTS):
@@ -287,14 +286,6 @@
     send_first(ORDER[-1])
     for tile in ORDER:
         send_near(0 if tile < HALF else 1, tile)
-    for tile in ORDER:
-        near_copy(0, tile).wait_recv()
-        near_copy(1, tile).wait_recv()
-        total = both(tile, 3) + (near_in[0, tile].astype(jnp.float32)
-                                 + near_in[1, tile].astype(jnp.float32))
-        result[:, tile * TILE:(tile + 1) * TILE] = total.astype(out.dtype)
-        out_copy(tile).start()
-
     for copy in own_copies(1):
         copy.wait_send()
     for copies in COPIES[2:]:
@@ -303,8 +294,18 @@
     for tile in range(TILES):
         for part in range(2):
             sib_copy(tile, part).wait_send()
-            near_copy(part, tile).wait_send()
         far_copy(tile).wait_send()
+        near_copy(0 if tile >= HALF else 1, tile).wait_send()
+    for tile in ORDER:
+        near_copy(0, tile).wait_recv()
+        near_copy(1, tile).wait_recv()
+        total = both(tile, 3) + (near_in[0, tile].astype(jnp.float32)
+                                 + near_in[1, tile].astype(jnp.float32))
+        result[:, tile * TILE:(tile + 1) * TILE] = total.astype(out.dtype)
+        out_copy(tile).start()
+
+    for tile in range(TILES):
+        near_copy(0 if tile < HALF else 1, tile).wait_send()
         out_copy(tile).wait()
 
 

time: 46.1 us -> 45.9 us (level)
  no operation moved by 1% of the time
where the time goes in v7:
time: 45.9 us
  Pallas kernels  45.1 us (98%)
  local copies, waits for them, and re-layouts  0.71 us (2%)
    pallas_call x1, Pallas kernels, on_device(): pl.pallas_call(kernel, out_shape=jax.ShapeDtypeStruct((rows // 8, d_out),...  45.1 us

profile of v7, /device:TPU:1, one launch (start us, length us, event | category | flops | bytes accessed | tf_op | source)
XLA Modules:
  0.0 45.9 jit_solution(1879474009704271264)
XLA Ops:
  0.0 45.1 %shard_map.55 = bf16[32,4096]{1,0:T(8,128)(2,1)S(1)} custom-call(s32[32]{0:T(128)} %order_hbm.1, bf16[256,1024]{1,0:T(8,128)(2,1)} %q_hbm.1, bf16[256,128]{1,0:T(8,128)(2,1)} %k_hbm.1, bf16[256,128]{1,0:T(8,128)(2,1)} %v_hbm.1, bf16[1024,4096]{1,0:T(8,128)(2,1)} %w_hbm.1), custom_call_target="tpu_custom_call" | custom-call | flops 6442450944 | bytes 10485760 | tf_op jit(solution)/shard_map/pallas_call | solution.py:321
  45.1 0.7 %copy.7 = bf16[32,4096]{1,0:T(8,128)(2,1)} copy(bf16[32,4096]{1,0:T(8,128)(2,1)S(1)} %shard_map.55) | data formatting | bytes 524288

commit v8 on v7

--- a/solution.py
+++ b/solution.py
@@ -188,9 +188,11 @@
         if head + 1 < heads:
             following = scores_of(keys, head + 1)
         new_top = jnp.max(scores, axis=0, keepdims=True)
+        if head:
+            acc[head - 1] = jnp.dot(values, weights, preferred_element_type=jnp.float32)
         weights = jnp.exp2(scores - new_top).astype(jnp.bfloat16)
         top[head] = new_top
-        acc[head] = jnp.dot(values, weights, preferred_element_type=jnp.float32)
+    acc[heads - 1] = jnp.dot(values, weights, preferred_element_type=jnp.float32)
 
     @pl.loop(0, ROUNDS)
     def _(step):
@@ -202,11 +204,18 @@
         first = 2 + 3 * step
         keys, values = operands(first, 3)
         hide = [jnp.where(span_of[first + number] < q_span, 0.0, LOWEST) for number in range(3)]
+
+        def add(head):
+            acc[head] = acc[head] * factor + jnp.dot(
+                values, weights, preferred_element_type=jnp.float32)
+
         following = scores_of(keys, 0)
         for head in range(heads):
             scores = [following[number * SPAN:(number + 1) * SPAN] for number in range(3)]
             if head + 1 < heads:
                 following = scores_of(keys, head + 1)
+            if head:
+                add(head - 1)
             old_top = top[head]
             new_top = old_top
             for part, hidden in zip(scores, hide):
@@ -216,8 +225,7 @@
                 jnp.exp2(part * scale - (new_top - hidden)).astype(jnp.bfloat16)
                 for part, hidden in zip(scores, hide)], axis=0)
             top[head] = new_top
-            acc[head] = acc[head] * factor + jnp.dot(
-                values, weights, preferred_element_type=jnp.float32)
+        add(heads - 1)
 
     for head in range(heads):
         mixed = acc[head, :HEAD_DIM] * (1.0 / acc[head, HEAD_DIM:HEAD_DIM + 1])

time: 45.9 us -> 46 us (level)
  no operation moved by 1% of the time
where the time goes in v8:
time: 46 us; the launch traced here: 45.9 us
  Pallas kernels  45.2 us (98%)
  local copies, waits for them, and re-layouts  0.71 us (2%)
    pallas_call x1, Pallas kernels, on_device(): pl.pallas_call(kernel, out_shape=jax.ShapeDtypeStruct((rows // 8, d_out),...  45.2 us

profile of v8, /device:TPU:1, one launch (start us, length us, event | category | flops | bytes accessed | tf_op | source)
XLA Modules:
  0.0 45.9 jit_solution(18263496504720946758)
XLA Ops:
  0.0 45.2 %shard_map.55 = bf16[32,4096]{1,0:T(8,128)(2,1)S(1)} custom-call(s32[32]{0:T(128)} %order_hbm.1, bf16[256,1024]{1,0:T(8,128)(2,1)} %q_hbm.1, bf16[256,128]{1,0:T(8,128)(2,1)} %k_hbm.1, bf16[256,128]{1,0:T(8,128)(2,1)} %v_hbm.1, bf16[1024,4096]{1,0:T(8,128)(2,1)} %w_hbm.1), custom_call_target="tpu_custom_call" | custom-call | flops 6442450944 | bytes 10485760 | tf_op jit(solution)/shard_map/pallas_call | solution.py:329
  45.2 0.7 %copy.7 = bf16[32,4096]{1,0:T(8,128)(2,1)} copy(bf16[32,4096]{1,0:T(8,128)(2,1)S(1)} %shard_map.55) | data formatting | bytes 524288

commit v9 on v7

--- a/solution.py
+++ b/solution.py
@@ -225,10 +225,16 @@
     loads[13].wait()
 
     def sib_copy(tile, part):
-        at = 0 if part == 0 else pl.ds(1, 3)
+        at = 0 if part == 0 else pl.ds(1, 2)
         return pltpu.make_async_remote_copy(
             src_ref=sib_out.at[tile, at], dst_ref=sib_in.at[tile, at],
             send_sem=sib_send.at[tile, part], recv_sem=sib_recv.at[tile, part],
+            device_id=sibling, device_id_type=MESH)
+
+    def home_copy():
+        return pltpu.make_async_remote_copy(
+            src_ref=sib_out.at[:, 3], dst_ref=sib_in.at[:, 3],
+            send_sem=sib_send.at[TILES, 0], recv_sem=sib_recv.at[TILES, 0],
             device_id=sibling, device_id_type=MESH)
 
     def project(tile):
@@ -284,6 +290,7 @@
         project(tile)
         send_first(earlier)
     send_first(ORDER[-1])
+    home_copy().start()
     for tile in ORDER:
         send_near(0 if tile < HALF else 1, tile)
     for copy in own_copies(1):
@@ -296,6 +303,7 @@
             sib_copy(tile, part).wait_send()
         far_copy(tile).wait_send()
         near_copy(0 if tile >= HALF else 1, tile).wait_send()
+    home_copy().wait()
     for tile in ORDER:
         near_copy(0, tile).wait_recv()
         near_copy(1, tile).wait_recv()
@@ -342,7 +350,7 @@
             pltpu.SMEM((SPANS,), jnp.int32),
             pltpu.SMEM((SPANS,), jnp.int32),
             sem((14,)), sem((6, 2)), sem((6, 2)), sem((SPANS - 8,)), sem((SPANS - 8,)),
-            sem((TILES, 2)), sem((TILES, 2)), sem((TILES,)), sem((TILES,)),
+            sem((TILES + 1, 2)), sem((TILES + 1, 2)), sem((TILES,)), sem((TILES,)),
             sem((2, TILES)), sem((2, TILES)), sem((TILES,)),
         ],
         compiler_params=pltpu.CompilerParams(

time: 45.9 us -> 45.9 us (level)
  no operation moved by 1% of the time
where the time goes in v9:
time: 45.9 us; the launch traced here: 45.8 us
  Pallas kernels  45.1 us (98%)
  local copies, waits for them, and re-layouts  0.71 us (2%)
    pallas_call x1, Pallas kernels, on_device(): pl.pallas_call(kernel, out_shape=jax.ShapeDtypeStruct((rows // 8, d_out),...  45.1 us

profile of v9, /device:TPU:1, one launch (start us, length us, event | category | flops | bytes accessed | tf_op | source)
XLA Modules:
  0.0 45.8 jit_solution(4967052670633489245)
XLA Ops:
  0.0 45.1 %shard_map.55 = bf16[32,4096]{1,0:T(8,128)(2,1)S(1)} custom-call(s32[32]{0:T(128)} %order_hbm.1, bf16[256,1024]{1,0:T(8,128)(2,1)} %q_hbm.1, bf16[256,128]{1,0:T(8,128)(2,1)} %k_hbm.1, bf16[256,128]{1,0:T(8,128)(2,1)} %v_hbm.1, bf16[1024,4096]{1,0:T(8,128)(2,1)} %w_hbm.1), custom_call_target="tpu_custom_call" | custom-call | flops 6442450944 | bytes 10485760 | tf_op jit(solution)/shard_map/pallas_call | solution.py:329
  45.1 0.7 %copy.7 = bf16[32,4096]{1,0:T(8,128)(2,1)} copy(bf16[32,4096]{1,0:T(8,128)(2,1)S(1)} %shard_map.55) | data formatting | bytes 524288

commit v10 on v9

--- a/solution.py
+++ b/solution.py
@@ -60,7 +60,7 @@
 
 
 def kernel(order_hbm, q_hbm, k_hbm, v_hbm, w_hbm, out,
-           q_in, kv, w, qt, acc, top, att, own, sib_out, sib_in,
+           q_in, kv, w, qt, acc, top, sums, att, own, sib_out, sib_in,
            far_out, far_in, near_out, near_in, result, order, span_of,
            load_sem, own_send, own_recv, kv_send, kv_recv, sib_send, sib_recv,
            far_send, far_recv, near_send, near_recv, out_sem):
@@ -152,9 +152,7 @@
     def operands(first, count):
         spans = kv[pl.ds(first, count)]
         keys = spans[:, 0].reshape(count * SPAN, HEAD_DIM)
-        values = spans[:, 1].reshape(count * SPAN, HEAD_DIM).T
-        ones = jnp.ones((16, count * SPAN), jnp.bfloat16)
-        return keys, jnp.concatenate([values, ones], axis=0)
+        return keys, spans[:, 1].reshape(count * SPAN, HEAD_DIM).T
 
     scale = math.log2(math.e) / math.sqrt(HEAD_DIM)
 
@@ -188,9 +186,10 @@
         if head + 1 < heads:
             following = scores_of(keys, head + 1)
         new_top = jnp.max(scores, axis=0, keepdims=True)
-        weights = jnp.exp2(scores - new_top).astype(jnp.bfloat16)
+        weights = jnp.exp2(scores - new_top)
         top[head] = new_top
-        acc[head] = jnp.dot(values, weights, preferred_element_type=jnp.float32)
+        sums[head] = jnp.sum(weights, axis=0, keepdims=True)
+        acc[head] = jnp.dot(values, weights.astype(jnp.bfloat16), preferred_element_type=jnp.float32)
 
     @pl.loop(0, ROUNDS)
     def _(step):
@@ -212,15 +211,17 @@
             for part, hidden in zip(scores, hide):
                 new_top = jnp.maximum(new_top, jnp.max(part, axis=0, keepdims=True) * scale + hidden)
             factor = jnp.exp2(old_top - new_top)
-            weights = jnp.concatenate([
-                jnp.exp2(part * scale - (new_top - hidden)).astype(jnp.bfloat16)
-                for part, hidden in zip(scores, hide)], axis=0)
+            weights = [jnp.exp2(part * scale - (new_top - hidden))
+                       for part, hidden in zip(scores, hide)]
             top[head] = new_top
+            sums[head] = sums[head] * factor + jnp.sum(
+                weights[0] + weights[1] + weights[2], axis=0, keepdims=True)
+            weights = jnp.concatenate([part.astype(jnp.bfloat16) for part in weights], axis=0)
             acc[head] = acc[head] * factor + jnp.dot(
                 values, weights, preferred_element_type=jnp.float32)
 
     for head in range(heads):
-        mixed = acc[head, :HEAD_DIM] * (1.0 / acc[head, HEAD_DIM:HEAD_DIM + 1])
+        mixed = acc[head] * (1.0 / sums[head])
         att[:, head * HEAD_DIM:(head + 1) * HEAD_DIM] = mixed.astype(jnp.bfloat16).T
     loads[13].wait()
 
@@ -336,7 +337,8 @@
             pltpu.VMEM((SPANS, 2, SPAN, HEAD_DIM), bf16),
             pltpu.VMEM((width, d_out), bf16),
             pltpu.VMEM((heads, HEAD_DIM, rows), bf16),
-            pltpu.VMEM((heads, HEAD_DIM + 16, rows), f32),
+            pltpu.VMEM((heads, HEAD_DIM, rows), f32),
+            pltpu.VMEM((heads, 1, rows), f32),
             pltpu.VMEM((heads, 1, rows), f32),
             pltpu.VMEM((rows, width), bf16),
             pltpu.VMEM((TILES, 4, 32, TILE), bf16),

time: 45.9 us -> 46.4 us (1.011)
  Pallas kernels: 45.1 us -> 45.7 us
    pallas_call x1, Pallas kernels: 45.1 us -> 45.7 us  [on_device(): pl.pallas_call(kernel, out_shape=jax.ShapeDtypeStruct((rows // 8, d_out),...]
where the time goes in v10:
time: 46.4 us
  Pallas kernels  45.7 us (98%)
  local copies, waits for them, and re-layouts  0.71 us (2%)
    pallas_call x1, Pallas kernels, on_device(): pl.pallas_call(kernel, out_shape=jax.ShapeDtypeStruct((rows // 8, d_out),...  45.7 us

profile of v10, /device:TPU:1, one launch (start us, length us, event | category | flops | bytes accessed | tf_op | source)
XLA Modules:
  0.0 46.4 jit_solution(957522921800590295)
XLA Ops:
  0.0 45.7 %shard_map.55 = bf16[32,4096]{1,0:T(8,128)(2,1)S(1)} custom-call(s32[32]{0:T(128)} %order_hbm.1, bf16[256,1024]{1,0:T(8,128)(2,1)} %q_hbm.1, bf16[256,128]{1,0:T(8,128)(2,1)} %k_hbm.1, bf16[256,128]{1,0:T(8,128)(2,1)} %v_hbm.1, bf16[1024,4096]{1,0:T(8,128)(2,1)} %w_hbm.1), custom_call_target="tpu_custom_call" | custom-call | flops 6442450944 | bytes 10485760 | tf_op jit(solution)/shard_map/pallas_call | solution.py:330
  45.7 0.7 %copy.7 = bf16[32,4096]{1,0:T(8,128)(2,1)} copy(bf16[32,4096]{1,0:T(8,128)(2,1)S(1)} %shard_map.55) | data formatting | bytes 524288

commit v11 on v9

--- a/solution.py
+++ b/solution.py
@@ -56,13 +56,14 @@
 
 CONTENTS, COPIES = plan()
 SPANS = len(CONTENTS)
+PAIRED = (0, 4, 2, 6)
 ORDER = tuple(part * HALF + tile for tile in range(HALF) for part in range(2))
 
 
 def kernel(order_hbm, q_hbm, k_hbm, v_hbm, w_hbm, out,
            q_in, kv, w, qt, acc, top, att, own, sib_out, sib_in,
            far_out, far_in, near_out, near_in, result, order, span_of,
-           load_sem, own_send, own_recv, kv_send, kv_recv, sib_send, sib_recv,
+           load_sem, kv_send, kv_recv, sib_send, sib_recv,
            far_send, far_recv, near_send, near_recv, out_sem):
     heads = q_in.shape[1] // HEAD_DIM
     rows = q_in.shape[0]
@@ -108,14 +109,20 @@
             for part, source in enumerate((k_hbm, v_hbm)):
                 yield pltpu.make_async_remote_copy(
                     src_ref=source.at[pl.ds(src * SPAN, SPAN)], dst_ref=kv.at[dst, part],
-                    send_sem=own_send.at[dst - 2, part], recv_sem=own_recv.at[dst - 2, part],
+                    send_sem=kv_send.at[r], recv_sem=kv_recv.at[r],
                     device_id=targets[name], device_id_type=MESH)
 
-    def copy_of(name, src, dst):
+    def copy_of(r, name, src, dst):
         return pltpu.make_async_remote_copy(
             src_ref=kv.at[src], dst_ref=kv.at[dst],
-            send_sem=kv_send.at[dst - 8], recv_sem=kv_recv.at[dst - 8],
+            send_sem=kv_send.at[r], recv_sem=kv_recv.at[r],
             device_id=targets[name], device_id_type=MESH)
+
+    def whole(r):
+        spans = kv.at[pl.ds(2 + 3 * r, 3)]
+        return pltpu.make_async_remote_copy(
+            src_ref=spans, dst_ref=spans, send_sem=kv_send.at[r], recv_sem=kv_recv.at[r],
+            device_id=targets["other"], device_id_type=MESH)
 
     pl.semaphore_wait(barrier, 6)
     for copy in own_copies(0):
@@ -133,9 +140,9 @@
     for head in range(heads):
         qt[head] = q_in[:, head * HEAD_DIM:(head + 1) * HEAD_DIM].T
 
-    for first, second in zip(own_copies(0), own_copies(1)):
-        first.wait_send()
-        second.start()
+    whole(0).wait_send()
+    for copy in own_copies(1):
+        copy.start()
     for load in loads[:4]:
         load.wait()
 
@@ -166,17 +173,11 @@
         here = 2 + 3 * r
         for copy in following:
             if copy[1] < here:
-                copy_of(*copy).start()
-        first = list(own_copies(r)) if r < 2 else ()
-        for number, copy in enumerate(COPIES[r]):
-            if r < 2:
-                first[2 * number].wait_recv()
-                first[2 * number + 1].wait_recv()
-            else:
-                copy_of(*copy).wait_recv()
-            for later in following:
-                if later[1] == copy[2]:
-                    copy_of(*later).start()
+                copy_of(r + 2, *copy).start()
+        whole(r).wait_recv()
+        for copy in following:
+            if copy[1] >= here:
+                copy_of(r + 2, *copy).start()
 
     keys, values = operands(0, 2)
     k_row = lax.broadcasted_iota(jnp.int32, (2 * SPAN, 1), 0)
@@ -224,17 +225,17 @@
         att[:, head * HEAD_DIM:(head + 1) * HEAD_DIM] = mixed.astype(jnp.bfloat16).T
     loads[13].wait()
 
-    def sib_copy(tile, part):
-        at = 0 if part == 0 else pl.ds(1, 2)
+    def sib_copy(tile):
+        at = pl.ds(0, 3)
         return pltpu.make_async_remote_copy(
             src_ref=sib_out.at[tile, at], dst_ref=sib_in.at[tile, at],
-            send_sem=sib_send.at[tile, part], recv_sem=sib_recv.at[tile, part],
+            send_sem=sib_send.at[tile], recv_sem=sib_recv.at[tile],
             device_id=sibling, device_id_type=MESH)
 
     def home_copy():
         return pltpu.make_async_remote_copy(
             src_ref=sib_out.at[:, 3], dst_ref=sib_in.at[:, 3],
-            send_sem=sib_send.at[TILES, 0], recv_sem=sib_recv.at[TILES, 0],
+            send_sem=sib_send.at[TILES], recv_sem=sib_recv.at[TILES],
             device_id=sibling, device_id_type=MESH)
 
     def project(tile):
@@ -242,8 +243,7 @@
                        preferred_element_type=jnp.float32).astype(jnp.bfloat16)
         part = part.reshape(4, 2, 32, TILE)
         sib_out[tile] = part[:, 1]
-        sib_copy(tile, 0).start()
-        sib_copy(tile, 1).start()
+        sib_copy(tile).start()
         own[tile] = part[:, 0]
 
     def both(tile, group):
@@ -255,9 +255,10 @@
             send_sem=far_send.at[tile], recv_sem=far_recv.at[tile],
             device_id=to_next if tile < HALF else to_back, device_id_type=MESH)
 
-    def near_copy(side, tile):
-        return pltpu.make_async_remote_copy(
-            src_ref=near_out.at[side, tile], dst_ref=near_in.at[side, tile],
+    def near_copy(side, tile, count):
+        at = pl.ds(tile, count)
+        return pltpu.make_async_remote_copy(
+            src_ref=near_out.at[side, at], dst_ref=near_in.at[side, at],
             send_sem=near_send.at[side, tile], recv_sem=near_recv.at[side, tile],
             device_id=to_next if side == 0 else to_back, device_id_type=MESH)
 
@@ -265,25 +266,24 @@
         at = pl.ds(tile * TILE, TILE)
         return pltpu.make_async_copy(result.at[:, at], out.at[:, at], out_sem.at[tile])
 
-    def send_far(tile):
-        sib_copy(tile, 0).wait_recv()
+    def first_side(tile):
+        return 0 if tile >= HALF else 1
+
+    def send_first(tile):
+        sib_copy(tile).wait_recv()
         far_out[tile] = both(tile, 0).astype(jnp.bfloat16)
         far_copy(tile).start()
-
-    def send_near(side, tile):
-        second = (tile < HALF) == (side == 0)
-        if not second:
-            sib_copy(tile, 1).wait_recv()
-        total = both(tile, 1 + side)
-        if second:
-            far_copy(tile).wait_recv()
-            total = total + far_in[tile].astype(jnp.float32)
-        near_out[side, tile] = total.astype(jnp.bfloat16)
-        near_copy(side, tile).start()
-
-    def send_first(tile):
-        send_far(tile)
-        send_near(0 if tile >= HALF else 1, tile)
+        side = first_side(tile)
+        near_out[side, tile] = both(tile, 1 + side).astype(jnp.bfloat16)
+        near_copy(side, tile, 1).start()
+
+    def send_second(tile):
+        side = 1 - first_side(tile)
+        for one in (tile, tile + 1):
+            far_copy(one).wait_recv()
+            total = both(one, 1 + side) + far_in[one].astype(jnp.float32)
+            near_out[side, one] = total.astype(jnp.bfloat16)
+        near_copy(side, tile, 2).start()
 
     project(ORDER[0])
     for earlier, tile in zip(ORDER, ORDER[1:]):
@@ -291,30 +291,28 @@
         send_first(earlier)
     send_first(ORDER[-1])
     home_copy().start()
-    for tile in ORDER:
-        send_near(0 if tile < HALF else 1, tile)
-    for copy in own_copies(1):
-        copy.wait_send()
-    for copies in COPIES[2:]:
-        for copy in copies:
-            copy_of(*copy).wait_send()
+    for tile in PAIRED:
+        send_second(tile)
+    for r in range(1, ROUNDS):
+        whole(r).wait_send()
     for tile in range(TILES):
-        for part in range(2):
-            sib_copy(tile, part).wait_send()
+        sib_copy(tile).wait_send()
         far_copy(tile).wait_send()
-        near_copy(0 if tile >= HALF else 1, tile).wait_send()
+        near_copy(first_side(tile), tile, 1).wait_send()
     home_copy().wait()
-    for tile in ORDER:
-        near_copy(0, tile).wait_recv()
-        near_copy(1, tile).wait_recv()
-        total = both(tile, 3) + (near_in[0, tile].astype(jnp.float32)
-                                 + near_in[1, tile].astype(jnp.float32))
-        result[:, tile * TILE:(tile + 1) * TILE] = total.astype(out.dtype)
-        out_copy(tile).start()
-
-    for tile in range(TILES):
-        near_copy(0 if tile < HALF else 1, tile).wait_send()
-        out_copy(tile).wait()
+    for pair in PAIRED:
+        near_copy(1 - first_side(pair), pair, 2).wait_recv()
+        for tile in (pair, pair + 1):
+            near_copy(first_side(tile), tile, 1).wait_recv()
+            total = both(tile, 3) + (near_in[0, tile].astype(jnp.float32)
+                                     + near_in[1, tile].astype(jnp.float32))
+            result[:, tile * TILE:(tile + 1) * TILE] = total.astype(out.dtype)
+            out_copy(tile).start()
+
+    for pair in PAIRED:
+        near_copy(1 - first_side(pair), pair, 2).wait_send()
+        for tile in (pair, pair + 1):
+            out_copy(tile).wait()
 
 
 def on_device(queries, keys, values, span_order, out_weight):
@@ -349,8 +347,8 @@
             pltpu.VMEM((rows // 8, d_out), bf16),
             pltpu.SMEM((SPANS,), jnp.int32),
             pltpu.SMEM((SPANS,), jnp.int32),
-            sem((14,)), sem((6, 2)), sem((6, 2)), sem((SPANS - 8,)), sem((SPANS - 8,)),
-            sem((TILES + 1, 2)), sem((TILES + 1, 2)), sem((TILES,)), sem((TILES,)),
+            sem((14,)), sem((ROUNDS,)), sem((ROUNDS,)),
+            sem((TILES + 1,)), sem((TILES + 1,)), sem((TILES,)), sem((TILES,)),
             sem((2, TILES)), sem((2, TILES)), sem((TILES,)),
         ],
         compiler_params=pltpu.CompilerParams(

time: 45.9 us -> 45.9 us (level)
  no operation moved by 1% of the time
where the time goes in v11:
time: 45.9 us; the launch traced here: 45.7 us
  Pallas kernels  45 us (98%)
  local copies, waits for them, and re-layouts  0.71 us (2%)
    pallas_call x1, Pallas kernels, on_device(): pl.pallas_call(kernel, out_shape=jax.ShapeDtypeStruct((rows // 8, d_out),...  45 us

profile of v11, /device:TPU:1, one launch (start us, length us, event | category | flops | bytes accessed | tf_op | source)
XLA Modules:
  0.0 45.7 jit_solution(16271188787223910403)
XLA Ops:
  0.0 45.0 %shard_map.55 = bf16[32,4096]{1,0:T(8,128)(2,1)S(1)} custom-call(s32[32]{0:T(128)} %order_hbm.1, bf16[256,1024]{1,0:T(8,128)(2,1)} %q_hbm.1, bf16[256,128]{1,0:T(8,128)(2,1)} %k_hbm.1, bf16[256,128]{1,0:T(8,128)(2,1)} %v_hbm.1, bf16[1024,4096]{1,0:T(8,128)(2,1)} %w_hbm.1), custom_call_target="tpu_custom_call" | custom-call | flops 6442450944 | bytes 10485760 | tf_op jit(solution)/shard_map/pallas_call | solution.py:327
  45.0 0.7 %copy.7 = bf16[32,4096]{1,0:T(8,128)(2,1)} copy(bf16[32,4096]{1,0:T(8,128)(2,1)S(1)} %shard_map.55) | data formatting | bytes 524288

commit v12 on v11

--- a/solution.py
+++ b/solution.py
@@ -238,13 +238,21 @@
             send_sem=sib_send.at[TILES], recv_sem=sib_recv.at[TILES],
             device_id=sibling, device_id_type=MESH)
 
+    def product(rows_from, rows_to, tile):
+        part = jnp.dot(att[rows_from:rows_to], w[:, tile * TILE:(tile + 1) * TILE],
+                       preferred_element_type=jnp.float32).astype(jnp.bfloat16)
+        return part.reshape(-1, 2, 32, TILE)
+
     def project(tile):
-        part = jnp.dot(att[...], w[:, tile * TILE:(tile + 1) * TILE],
-                       preferred_element_type=jnp.float32).astype(jnp.bfloat16)
-        part = part.reshape(4, 2, 32, TILE)
-        sib_out[tile] = part[:, 1]
+        part = product(0, 192, tile)
+        sib_out[tile, :3] = part[:, 1]
         sib_copy(tile).start()
-        own[tile] = part[:, 0]
+        own[tile, :3] = part[:, 0]
+
+    def project_home(tile):
+        part = product(192, 256, tile)
+        sib_out[tile, 3] = part[0, 1]
+        own[tile, 3] = part[0, 0]
 
     def both(tile, group):
         return own[tile, group].astype(jnp.float32) + sib_in[tile, group].astype(jnp.float32)
@@ -290,8 +298,12 @@
         project(tile)
         send_first(earlier)
     send_first(ORDER[-1])
+    for tile in PAIRED[:2]:
+        send_second(tile)
+    for tile in ORDER:
+        project_home(tile)
     home_copy().start()
-    for tile in PAIRED:
+    for tile in PAIRED[2:]:
         send_second(tile)
     for r in range(1, ROUNDS):
         whole(r).wait_send()

time: 45.9 us -> 45.7 us (level)
  no operation moved by 1% of the time
where the time goes in v12:
time: 45.7 us; the launch traced here: 45.5 us
  Pallas kernels  44.8 us (98%)
  local copies, waits for them, and re-layouts  0.71 us (2%)
    pallas_call x1, Pallas kernels, on_device(): pl.pallas_call(kernel, out_shape=jax.ShapeDtypeStruct((rows // 8, d_out),...  44.8 us

profile of v12, /device:TPU:1, one launch (start us, length us, event | category | flops | bytes accessed | tf_op | source)
XLA Modules:
  0.0 45.5 jit_solution(5386355122926869479)
XLA Ops:
  0.0 44.8 %shard_map.55 = bf16[32,4096]{1,0:T(8,128)(2,1)S(1)} custom-call(s32[32]{0:T(128)} %order_hbm.1, bf16[256,1024]{1,0:T(8,128)(2,1)} %q_hbm.1, bf16[256,128]{1,0:T(8,128)(2,1)} %k_hbm.1, bf16[256,128]{1,0:T(8,128)(2,1)} %v_hbm.1, bf16[1024,4096]{1,0:T(8,128)(2,1)} %w_hbm.1), custom_call_target="tpu_custom_call" | custom-call | flops 6442450944 | bytes 10485760 | tf_op jit(solution)/shard_map/pallas_call | solution.py:339
  44.8 0.7 %copy.7 = bf16[32,4096]{1,0:T(8,128)(2,1)} copy(bf16[32,4096]{1,0:T(8,128)(2,1)S(1)} %shard_map.55) | data formatting | bytes 524288

commit v13 on v12

--- a/solution.py
+++ b/solution.py
@@ -140,7 +140,6 @@
     for head in range(heads):
         qt[head] = q_in[:, head * HEAD_DIM:(head + 1) * HEAD_DIM].T
 
-    whole(0).wait_send()
     for copy in own_copies(1):
         copy.start()
     for load in loads[:4]:
@@ -305,7 +304,7 @@
     home_copy().start()
     for tile in PAIRED[2:]:
         send_second(tile)
-    for r in range(1, ROUNDS):
+    for r in range(ROUNDS):
         whole(r).wait_send()
     for tile in range(TILES):
         sib_copy(tile).wait_send()

time: 45.7 us -> 46 us (level)
  no operation moved by 1% of the time
where the time goes in v13:
time: 46 us; the launch traced here: 45.8 us
  Pallas kernels  45 us (98%)
  local copies, waits for them, and re-layouts  0.71 us (2%)
    pallas_call x1, Pallas kernels, on_device(): pl.pallas_call(kernel, out_shape=jax.ShapeDtypeStruct((rows // 8, d_out),...  45 us

profile of v13, /device:TPU:1, one launch (start us, length us, event | category | flops | bytes accessed | tf_op | source)
XLA Modules:
  0.0 45.8 jit_solution(16675012693348129851)
XLA Ops:
  0.0 45.0 %shard_map.55 = bf16[32,4096]{1,0:T(8,128)(2,1)S(1)} custom-call(s32[32]{0:T(128)} %order_hbm.1, bf16[256,1024]{1,0:T(8,128)(2,1)} %q_hbm.1, bf16[256,128]{1,0:T(8,128)(2,1)} %k_hbm.1, bf16[256,128]{1,0:T(8,128)(2,1)} %v_hbm.1, bf16[1024,4096]{1,0:T(8,128)(2,1)} %w_hbm.1), custom_call_target="tpu_custom_call" | custom-call | flops 6442450944 | bytes 10485760 | tf_op jit(solution)/shard_map/pallas_call | solution.py:338
  45.1 0.7 %copy.7 = bf16[32,4096]{1,0:T(8,128)(2,1)} copy(bf16[32,4096]{1,0:T(8,128)(2,1)S(1)} %shard_map.55) | data formatting | bytes 524288
